TPU v7x, 32 devices: a whole 2x2x4 slice. The times are simulated.
32 devices in a mesh: tensor: 4 (over y, core), dp: 8 (over z, x).
Axes of the slice: x: 2, y: 2, z: 4, core: 2. Of those that a mesh axis runs over, the one named last changes fastest.
Arguments:
- inputs: bfloat16 [4096, 512], P('dp'), may hold values from -6 to 6
- norm_gains: bfloat16 [5, 512], replicated, may hold values from 0.25 to 1.75
- early_up: bfloat16 [512, 2048], P(None, 'tensor'), may hold values from -0.25 to 0.25
- early_down: bfloat16 [2048, 512], P('tensor'), may hold values from -0.25 to 0.25
- query_key_value: bfloat16 [512, 3, 512], P(None, None, 'tensor'), may hold values from -0.25 to 0.25
- position_weight: bfloat16 [512, 512], P(None, 'tensor'), may hold values from -0.25 to 0.25
- position_bias: bfloat16 [2, 8, 64], P(None, 'tensor'), may hold values from -3 to 3
- attention_out: bfloat16 [512, 512], P('tensor'), may hold values from -0.75 to 0.75
- pointwise_in: bfloat16 [512, 2, 512], P(None, None, 'tensor'), may hold values from -0.25 to 0.25
- depthwise: bfloat16 [31, 512], P(None, 'tensor'), may hold values from -1 to 1
- batch_gain: bfloat16 [512], P('tensor'), may hold values from 0.25 to 1.75
- batch_bias: bfloat16 [512], P('tensor'), may hold values from -3 to 3
- pointwise_out: bfloat16 [512, 512], P('tensor'), may hold values from -0.375 to 0.375
- late_up: bfloat16 [512, 2048], P(None, 'tensor'), may hold values from -0.25 to 0.25
- late_down: bfloat16 [2048, 512], P('tensor'), may hold values from -0.25 to 0.25
- output_cotangent: bfloat16 [4096, 512], P('dp'), may hold values from -6 to 6
Outputs:
- layer_output: bfloat16 [4096, 512], P('dp')
- input_gradient: float32 [4096, 512], P('dp')
- gains_gradient: float32 [5, 512], replicated
- early_up_gradient: float32 [512, 2048], P(None, 'tensor')
- early_down_gradient: float32 [2048, 512], P('tensor')
- query_key_value_gradient: float32 [512, 3, 512], P(None, None, 'tensor')
- position_weight_gradient: float32 [512, 512], P(None, 'tensor')
- position_bias_gradient: float32 [2, 8, 64], P(None, 'tensor')
- attention_out_gradient: float32 [512, 512], P('tensor')
- pointwise_in_gradient: float32 [512, 2, 512], P(None, None, 'tensor')
- depthwise_gradient: float32 [31, 512], P(None, 'tensor')
- batch_gain_gradient: float32 [512], P('tensor')
- batch_bias_gradient: float32 [512], P('tensor')
- pointwise_out_gradient: float32 [512, 512], P('tensor')
- late_up_gradient: float32 [512, 2048], P(None, 'tensor')
- late_down_gradient: float32 [2048, 512], P('tensor')
All inputs are finite; a program needn't handle non-finite values.
Results may differ from a plain program's by a relative error of at most 0.02.
Values sent between devices are 32-bit elements; how exact they have to be, the bound alone decides.
A program may use at most 128 MiB of HBM per device.

v0:
```python
import math
import jax
import jax.numpy as jnp
from jax import lax
from jax.sharding import PartitionSpec as P

LENGTH = 512
EPS = 1e-05


def plain_round(v):
    return lax.optimization_barrier(v.astype(jnp.bfloat16)).astype(jnp.float32)


def plain_same(v):
    return v


def value_keep(v):
    return (plain_round(v), None)


def value_pass(kept, grad):
    return (grad,)


def grad_keep(v):
    return (v, None)


def grad_round(kept, grad):
    return (plain_round(grad),)


def low(v):
    rounder = jax.custom_vjp(plain_round)
    rounder.defvjp(value_keep, value_pass)
    return rounder(v)


def low_back(v):
    rounder = jax.custom_vjp(plain_same)
    rounder.defvjp(grad_keep, grad_round)
    return rounder(v)


def matmul(first_factor, second_factor):
    return jnp.dot(first_factor, second_factor, preferred_element_type=jnp.float32)


def layer_norm(values, gain_row):
    centre = values - jnp.mean(values, axis=-1, keepdims=True)
    spread = jnp.mean(centre * centre, axis=-1, keepdims=True)
    return centre * lax.rsqrt(spread + EPS) * gain_row


def sinusoid_table(length, model_width):
    offsets = (length - 1 - jnp.arange(2 * length - 1)).astype(jnp.float32)
    frequency = jnp.exp(
        jnp.arange(0, model_width, 2).astype(jnp.float32) * (-math.log(10000.0) / model_width)
    )
    phases = offsets[:, None] * frequency[None, :]
    return jnp.stack([jnp.sin(phases), jnp.cos(phases)], axis=-1).reshape(
        2 * length - 1, model_width
    )


def relative_shift(scores):
    head_count, length, span_size = scores.shape
    padded = jnp.pad(scores, ((0, 0), (0, 0), (1, 0)))
    padded = padded.reshape(head_count, 2 * length, length)[:, 1:]
    return padded.reshape(head_count, length, span_size)[:, :, :length]


def feed_forward(values, gain_row, weight_in, weight_out):
    normed = low(layer_norm(values, gain_row))
    hidden = low_back(matmul(normed, weight_in))
    active = low(jax.nn.silu(hidden))
    return low_back(matmul(active, weight_out))


def sequence_core(sequence, sinusoid, weight_pos, biases):
    length = sequence.shape[0]
    head_count = sequence.shape[2]
    head_size = sequence.shape[3]
    queries = sequence[:, 0]
    key_rows = low(sequence[:, 1])
    values = low(sequence[:, 2])
    position = low(low_back(matmul(sinusoid, weight_pos))).reshape(
        2 * length - 1, head_count, head_size
    )
    with_content = low(queries + biases[0])
    with_position = low(queries + biases[1])
    content = jnp.einsum("ihd,jhd->hij", with_content, key_rows, preferred_element_type=jnp.float32)
    relative = relative_shift(
        jnp.einsum("ihd,rhd->hir", with_position, position, preferred_element_type=jnp.float32)
    )
    scores = low_back((content + relative) * (1.0 / math.sqrt(head_size)))
    weights = low(jax.nn.softmax(scores, axis=-1))
    return jnp.einsum("hij,jhd->ihd", weights, values, preferred_element_type=jnp.float32)


def attention(values, gain_row, weight_qkv, weight_pos, biases, weight_out):
    model_width = weight_qkv.shape[0]
    local_width = weight_qkv.shape[2]
    head_count = biases.shape[1]
    head_size = biases.shape[2]
    normed = low(layer_norm(values, gain_row))
    mixed_rows = low_back(matmul(normed, weight_qkv.reshape(model_width, 3 * local_width)))
    mixed_rows = mixed_rows.reshape(-1, LENGTH, 3, head_count, head_size)
    sinusoid = low(sinusoid_table(LENGTH, model_width))
    per_sequence = jax.checkpoint(
        lambda sequence: sequence_core(sequence, sinusoid, weight_pos, biases)
    )
    attended = lax.map(per_sequence, mixed_rows).reshape(-1, local_width)
    attended = low(low_back(attended))
    return low_back(matmul(attended, weight_out))


def depthwise_conv(gated, kernel):
    half = kernel.shape[0] // 2
    return lax.conv_general_dilated(
        gated,
        kernel[:, None, :],
        (1,),
        [(half, half)],
        dimension_numbers=("NWC", "WIO", "NWC"),
        feature_group_count=gated.shape[2],
        precision=lax.Precision.HIGHEST,
    )


def conv_front(values, gain_row, weight_in, kernel):
    channels = kernel.shape[1]
    normed = low(layer_norm(values, gain_row))
    paired = low_back(matmul(normed, weight_in.reshape(weight_in.shape[0], 2 * channels))).reshape(
        -1, 2, channels
    )
    gated = paired[:, 0] * jax.nn.sigmoid(paired[:, 1])
    return depthwise_conv(gated.reshape(-1, LENGTH, channels), kernel)


def conv_back(mixed_rows, batch_mean, batch_var, scale_row, shift_row, weight_out):
    scaled = (mixed_rows - batch_mean) * lax.rsqrt(batch_var + EPS) * scale_row + shift_row
    swished = low(jax.nn.silu(scaled)).reshape(-1, mixed_rows.shape[2])
    return low_back(matmul(swished, weight_out))


def add_branch(base_rows, partial_value, factor):
    return base_rows + factor * lax.psum(partial_value, "tensor")


def add_gradient(base_rows, cotangent_in, gain_piece):
    cotangent_sum, gain_total = lax.psum((cotangent_in, gain_piece), "tensor")
    return (base_rows + cotangent_sum, gain_total)


def per_device(
    inputs,
    norm_gains,
    early_up,
    early_down,
    query_key_value,
    position_weight,
    position_bias,
    attention_out,
    pointwise_in,
    depthwise,
    batch_gain,
    batch_bias,
    pointwise_out,
    late_up,
    late_down,
    output_cotangent,
):
    stream = inputs.astype(jnp.float32)
    gain_rows = norm_gains.astype(jnp.float32)
    early_in = early_up.astype(jnp.float32)
    early_back = early_down.astype(jnp.float32)
    project_qkv = query_key_value.astype(jnp.float32)
    project_pos = position_weight.astype(jnp.float32)
    query_bias = position_bias.astype(jnp.float32)
    project_out = attention_out.astype(jnp.float32)
    point_first = pointwise_in.astype(jnp.float32)
    depth_taps = depthwise.astype(jnp.float32)
    scale_row = batch_gain.astype(jnp.float32)
    shift_row = batch_bias.astype(jnp.float32)
    point_second = pointwise_out.astype(jnp.float32)
    late_in = late_up.astype(jnp.float32)
    late_back = late_down.astype(jnp.float32)
    first_part, first_pull = jax.vjp(feed_forward, stream, gain_rows[0], early_in, early_back)
    after_first = add_branch(stream, first_part, 0.5)
    second_part, second_pull = jax.vjp(
        attention, after_first, gain_rows[1], project_qkv, project_pos, query_bias, project_out
    )
    after_second = add_branch(after_first, second_part, 1.0)
    mixed_rows, front_pull = jax.vjp(
        conv_front, after_second, gain_rows[2], point_first, depth_taps
    )
    token_count = mixed_rows.shape[0] * mixed_rows.shape[1] * lax.axis_size("dp")
    sum_values, sum_squares = lax.psum(
        (jnp.sum(mixed_rows, axis=(0, 1)), jnp.sum(mixed_rows * mixed_rows, axis=(0, 1))), "dp"
    )
    batch_mean = sum_values / token_count
    batch_var = sum_squares / token_count - batch_mean * batch_mean
    third_part, back_pull = jax.vjp(
        conv_back, mixed_rows, batch_mean, batch_var, scale_row, shift_row, point_second
    )
    after_third = add_branch(after_second, third_part, 1.0)
    fourth_part, fourth_pull = jax.vjp(feed_forward, after_third, gain_rows[3], late_in, late_back)
    after_fourth = add_branch(after_third, fourth_part, 0.5)
    result, final_pull = jax.vjp(layer_norm, after_fourth, gain_rows[4])
    grad_four, final_gain = final_pull(output_cotangent.astype(jnp.float32))
    cotangent_in, gain_piece, late_in_grad, late_back_grad = fourth_pull(0.5 * grad_four)
    grad_three, gain_four = add_gradient(grad_four, cotangent_in, gain_piece)
    final_gain, gain_four, late_in_grad, late_back_grad = (
        final_gain,
        gain_four,
        late_in_grad,
        late_back_grad,
    )
    direct_grad, mean_grad, var_grad, scale_grad, shift_grad, second_point_grad = back_pull(
        grad_three
    )
    mean_grad, var_grad = lax.psum((mean_grad, var_grad), "dp")
    mixed_grad = (
        direct_grad + (mean_grad + 2.0 * var_grad * (mixed_rows - batch_mean)) / token_count
    )
    cotangent_in, gain_piece, first_point_grad, depth_grad = front_pull(mixed_grad)
    grad_two, gain_two = add_gradient(grad_three, cotangent_in, gain_piece)
    gain_two, scale_grad, shift_grad, second_point_grad, first_point_grad, depth_grad = (
        gain_two,
        scale_grad,
        shift_grad,
        second_point_grad,
        first_point_grad,
        depth_grad,
    )
    cotangent_in, gain_piece, qkv_grad, pos_grad, bias_grad, out_grad = second_pull(grad_two)
    grad_one, gain_one = add_gradient(grad_two, cotangent_in, gain_piece)
    gain_one, qkv_grad, pos_grad, bias_grad, out_grad = (
        gain_one,
        qkv_grad,
        pos_grad,
        bias_grad,
        out_grad,
    )
    cotangent_in, gain_piece, early_in_grad, early_back_grad = first_pull(0.5 * grad_one)
    grad_zero, gain_zero = add_gradient(grad_one, cotangent_in, gain_piece)
    gain_zero, early_in_grad, early_back_grad = (gain_zero, early_in_grad, early_back_grad)
    gain_grads = jnp.stack([gain_zero, gain_one, gain_two, gain_four, final_gain])
    (
        gain_grads,
        early_in_grad,
        early_back_grad,
        qkv_grad,
        pos_grad,
        bias_grad,
        out_grad,
        first_point_grad,
        depth_grad,
        scale_grad,
        shift_grad,
        second_point_grad,
        late_in_grad,
        late_back_grad,
    ) = lax.psum(
        (
            gain_grads,
            early_in_grad,
            early_back_grad,
            qkv_grad,
            pos_grad,
            bias_grad,
            out_grad,
            first_point_grad,
            depth_grad,
            scale_grad,
            shift_grad,
            second_point_grad,
            late_in_grad,
            late_back_grad,
        ),
        "dp",
    )
    return (
        result.astype(jnp.bfloat16),
        grad_zero,
        gain_grads,
        early_in_grad,
        early_back_grad,
        qkv_grad,
        pos_grad,
        bias_grad,
        out_grad,
        first_point_grad,
        depth_grad,
        scale_grad,
        shift_grad,
        second_point_grad,
        late_in_grad,
        late_back_grad,
    )


def solution(mesh):
    return jax.shard_map(
        per_device,
        mesh=mesh,
        in_specs=(
            P("dp", None),
            P(),
            P(None, "tensor"),
            P("tensor", None),
            P(None, None, "tensor"),
            P(None, "tensor"),
            P(None, "tensor", None),
            P("tensor", None),
            P(None, None, "tensor"),
            P(None, "tensor"),
            P("tensor"),
            P("tensor"),
            P("tensor", None),
            P(None, "tensor"),
            P("tensor", None),
            P("dp", None),
        ),
        out_specs=(
            P("dp", None),
            P("dp", None),
            P(),
            P(None, "tensor"),
            P("tensor", None),
            P(None, None, "tensor"),
            P(None, "tensor"),
            P(None, "tensor", None),
            P("tensor", None),
            P(None, None, "tensor"),
            P(None, "tensor"),
            P("tensor"),
            P("tensor"),
            P("tensor", None),
            P(None, "tensor"),
            P("tensor", None),
        ),
        check_vma=False,
    )
```

profile of v0, /device:TPU:0, one launch (start us, length us, event | category | flops | bytes accessed | tf_op | source)
XLA Modules:
  0.0 733.0 jit_solution(10238060074771365690)
XLA Ops:
  17.1 31.0 %fusion.20 = (bf16[1023,256,1]{0,2,1:T(2,128)(2,1)S(1)}, bf16[1023,256,1]{0,2,1:T(2,128)(2,1)S(1)}) fusion(f32[1023]{0:T(1024)S(1)} %subtract_convert_fusion, f32[256]{0:T(256)S(1)} %multiply_exponential_fusion), kind=kLoop, calls=%fused_computation.49 | loop fusion | flops 785664 | bytes 1052668 | tf_op jit(solution)/shard_map/convert.3
  48.1 2.5 pad_maximum_fusion
  59.9 3.2 pad.50
  63.1 5.0 reshape.456
  68.1 4.9 slice.118
  73.0 6.5 reshape.457
  79.5 3.1 slice.119
  82.6 2.9 copy.109
  85.5 3.8 fusion.102
  94.2 37.0 %all-reduce.28.cloned.1.call-done = f32[512,512]{1,0:T(8,128)} async-done(((f32[512,512]{1,0:T(8,128)}), f32[512,512]{1,0:T(8,128)}) %all-reduce.28.cloned.1.call-update) | async-done | bytes 1048592 | tf_op jit(solution)/shard_map/psum | solution.py:150
  134.6 21.5 %all-reduce.13 = (f32[128]{0:T(128)S(1)}, f32[128]{0:T(128)S(1)}) all-reduce(f32[128]{0:T(128)S(1)} %get-tuple-element.85, f32[128]{0:T(128)S(1)} %get-tuple-element.84), channel_id=1, replica_groups=mesh['tensor'=4,'dp'=8] {'dp'}, use_global_device_ids=true, to_apply=%region_11.12 | all-reduce | flops 256 | bytes 2048 | tf_op jit(solution)/shard_map/psum | solution.py:201
  159.8 32.9 %all-reduce.30.cloned.1.call-done = f32[512,512]{1,0:T(8,128)} async-done(((f32[512,512]{1,0:T(8,128)}), f32[512,512]{1,0:T(8,128)}) %all-reduce.30.cloned.1.call-update) | async-done | bytes 1048592 | tf_op jit(solution)/shard_map/psum | solution.py:150
  199.7 36.5 %all-reduce.32.cloned.1.call-done = f32[512,512]{1,0:T(8,128)} async-done(((f32[512,512]{1,0:T(8,128)}), f32[512,512]{1,0:T(8,128)}) %all-reduce.32.cloned.1.call-update) | async-done | bytes 1048592 | tf_op jit(solution)/shard_map/psum | solution.py:150
  253.0 2.5 fusion.117
  255.5 25.7 %all-reduce.34.cloned.1.call-done = f32[512,512]{1,0:T(8,128)} async-done(((f32[512,512]{1,0:T(8,128)}), f32[512,512]{1,0:T(8,128)}) %all-reduce.34.cloned.1.call-update) | async-done | bytes 1048592 | tf_op jit(solution)/shard_map/psum | solution.py:154
  285.5 22.0 %all-reduce.12 = (f32[128]{0:T(128)}, f32[128]{0:T(128)}) all-reduce(f32[128]{0:T(128)} %neg.55, f32[128]{0:T(128)} %multiply_multiply_fusion.5), channel_id=1, replica_groups=mesh['tensor'=4,'dp'=8] {'dp'}, use_global_device_ids=true, to_apply=%region_26.27 | all-reduce | flops 256 | bytes 2048 | tf_op jit(solution)/shard_map/psum | solution.py:225
  320.7 2.7 fusion.116
  327.5 25.9 %all-reduce.36.cloned.1.call-done = f32[512,512]{1,0:T(8,128)} async-done(((f32[512,512]{1,0:T(8,128)}), f32[512,512]{1,0:T(8,128)}) %all-reduce.36.cloned.1.call-update) | async-done | bytes 1048592 | tf_op jit(solution)/shard_map/psum | solution.py:154
  353.4 2.7 fusion.89
  362.4 3.2 pad.53
  365.6 5.0 reshape.463
  370.5 4.9 slice.135
  375.4 6.5 reshape.464
  385.4 2.7 fusion.103
  396.1 6.1 reshape.465
  404.1 2.9 reshape.466
  419.0 30.1 %all-reduce.38.cloned.1.call-done = f32[512,512]{1,0:T(8,128)} async-done(((f32[512,512]{1,0:T(8,128)}), f32[512,512]{1,0:T(8,128)}) %all-reduce.38.cloned.1.call-update) | async-done | bytes 1048592 | tf_op jit(solution)/shard_map/psum | solution.py:154
  458.8 5.9 fusion.106
  464.7 6.3 all-reduce.15
  471.1 38.5 %all-reduce.11 = (f32[5,512]{1,0:T(8,128)}, f32[2,2,64]{2,1,0:T(2,128)}, f32[31,128]{1,0:T(8,128)}, f32[128]{0:T(128)}, f32[128]{0:T(128)}) all-reduce(f32[5,512]{1,0:T(8,128)S(1)} %stack.27, f32[2,2,64]{2,1,0:T(2,128)S(1)} %pad_add_fusion, f32[31,128]{1,0:T(8,128)S(1)} %bitcast.232, ...), channel_id=1, replica_groups=mesh['tensor'=4,'dp'=8] {'dp'}, use_global_device_ids=true, to_apply=%region_50.51 | all-reduce | flops 7040 | bytes 56320 | tf_op jit(solution)/shard_map/psum | solution.py:267
  509.6 2.4 add.310
  512.0 204.9 %all-reduce.42.cloned.1.call-done = (f32[512,512]{1,0:T(8,128)}, f32[512,512]{1,0:T(8,128)}, f32[512,3,128]{2,0,1:T(8,128)}, f32[512,128]{1,0:T(8,128)}, f32[128...) async-done(((f32[512,512]{1,0:T(8,128)}, f32[512,512]{1,0:T(8,128)}, f32[512,3,128]{2,0,1:T(8,128)}, ...) | async-done | bytes 6291472 | tf_op jit(solution)/shard_map/psum | solution.py:267
  (457 shorter events, 125.5 us)
Async XLA Ops:
  7.2 188.7 %copy-start = (bf16[512,512]{1,0:T(8,128)(2,1)S(1)}, bf16[512,512]{1,0:T(8,128)(2,1)}, u32[]{:S(2)}) copy-start(bf16[512,512]{1,0:T(8,128)(2,1)} %param.29) | copy-start | bytes 1572868
  7.2 6.1 copy-start.70
  7.2 48.8 %all-reduce.26.cloned.1.call-start = ((), (), s32[]{:S(2)}) async-start(), calls=%async_computation | async-start | bytes 2097152 | tf_op jit(solution)/shard_map/psum | solution.py:150
  8.6 6.2 copy-start.79
  12.0 45.8 %copy-start.110 = (f32[1,512]{1,0:T(1,128)}, f32[1,512]{1,0:T(1,128)S(1)}, u32[]{:S(2)}) copy-start(f32[1,512]{1,0:T(1,128)S(1)} %get-tuple-element.159) | copy-start | bytes 6148
  12.0 120.9 %copy-start.93 = (f32[1,512]{1,0:T(1,128)}, f32[1,512]{1,0:T(1,128)S(1)}, u32[]{:S(2)}) copy-start(f32[1,512]{1,0:T(1,128)S(1)} %get-tuple-element.158) | copy-start | bytes 6148
  17.0 114.1 %all-reduce.28.cloned.1.call-start = ((), (), s32[]{:S(2)}) async-start(), calls=%async_computation.1 | async-start | bytes 2097152 | tf_op jit(solution)/shard_map/psum | solution.py:150
  50.8 7.5 %copy-start.38 = (bf16[512,3,128]{0,2,1:T(8,128)(2,1)}, bf16[512,3,128]{0,2,1:T(8,128)(2,1)S(1)}, u32[]{:S(2)}) copy-start(bf16[512,3,128]{0,2,1:T(8,128)(2,1)S(1)} %copy.60) | copy-start | bytes 1179652
  51.7 5.8 copy-start.5
  57.4 73.7 %copy-start.2 = (f32[512,512]{1,0:T(8,128)}, f32[512,512]{1,0:T(8,128)S(1)}, u32[]{:S(2)}) copy-start(f32[512,512]{1,0:T(8,128)S(1)} %get-tuple-element.137) | copy-start | bytes 3145732
  93.5 99.2 %all-reduce.30.cloned.1.call-start = ((), (), s32[]{:S(2)}) async-start(), calls=%async_computation.2 | async-start | bytes 2097152 | tf_op jit(solution)/shard_map/psum | solution.py:150
  94.0 62.7 %copy-start.120 = (f32[128]{0:T(128)}, f32[128]{0:T(128)S(1)}, u32[]{:S(2)}) copy-start(f32[128]{0:T(128)S(1)} %convert_element_type.256) | copy-start | bytes 1540
  134.6 23.8 %copy-start.57 = (bf16[128,512]{1,0:T(8,128)(2,1)S(1)}, bf16[128,512]{1,0:T(8,128)(2,1)}, u32[]{:S(2)}) copy-start(bf16[128,512]{1,0:T(8,128)(2,1)} %param.28) | copy-start | bytes 393220
  159.8 76.5 %all-reduce.32.cloned.1.call-start = ((), (), s32[]{:S(2)}) async-start(), calls=%async_computation.3 | async-start | bytes 2097152 | tf_op jit(solution)/shard_map/psum | solution.py:150
  199.6 81.6 %all-reduce.34.cloned.1.call-start = ((), (), s32[]{:S(2)}) async-start(), calls=%async_computation.4 | async-start | bytes 2097152 | tf_op jit(solution)/shard_map/psum | solution.py:154
  244.6 108.8 %all-reduce.36.cloned.1.call-start = ((), (), s32[]{:S(2)}) async-start(), calls=%async_computation.5 | async-start | bytes 2097152 | tf_op jit(solution)/shard_map/psum | solution.py:154
  245.5 7.5 %copy-start.31 = (bf16[512,512]{1,0:T(8,128)(2,1)S(1)}, bf16[512,512]{1,0:T(8,128)(2,1)}, u32[]{:S(2)}) copy-start(bf16[512,512]{1,0:T(8,128)(2,1)} %copy-done.30) | copy-start | bytes 1572868
  247.0 34.2 %copy-start.9 = (f32[512,512]{1,0:T(8,128)S(1)}, f32[512,512]{1,0:T(8,128)}, u32[]{:S(2)}) copy-start(f32[512,512]{1,0:T(8,128)} %copy-done.8) | copy-start | bytes 3145732
  282.9 28.8 %copy-start.15 = (bf16[512,512]{1,0:T(8,128)(2,1)}, bf16[512,512]{1,0:T(8,128)(2,1)S(1)}, u32[]{:S(2)}) copy-start(bf16[512,512]{1,0:T(8,128)(2,1)S(1)} %fusion.67) | copy-start | bytes 1572868
  320.4 6.1 copy-start.16
  320.4 128.6 %all-reduce.38.cloned.1.call-start = ((), (), s32[]{:S(2)}) async-start(), calls=%async_computation.6 | async-start | bytes 2097152 | tf_op jit(solution)/shard_map/psum | solution.py:154
  323.4 30.1 %copy-start.92 = (f32[512]{0:T(512)S(1)}, f32[512]{0:T(512)}, u32[]{:S(2)}) copy-start(f32[512]{0:T(512)} %copy-done.91) | copy-start | bytes 6148
  327.5 29.4 %copy-start.61 = (bf16[128,512]{1,0:T(8,128)(2,1)S(1)}, bf16[128,512]{1,0:T(8,128)(2,1)}, u32[]{:S(2)}) copy-start(bf16[128,512]{1,0:T(8,128)(2,1)} %param.23) | copy-start | bytes 393220
  327.5 29.9 %copy-start.109 = (f32[2,2,64]{2,1,0:T(2,128)S(1)}, f32[2,2,64]{2,1,0:T(2,128)}, u32[]{:S(2)}) copy-start(f32[2,2,64]{2,1,0:T(2,128)} %copy-done.108) | copy-start | bytes 3076
  412.4 97.2 %all-reduce.40.cloned.1.call-start = ((), (), s32[]{:S(2)}) async-start(), calls=%async_computation.7 | async-start | bytes 2097152 | tf_op jit(solution)/shard_map/psum | solution.py:154
  417.9 31.2 %copy-start.21 = (f32[512,512]{1,0:T(8,128)S(1)}, f32[512,512]{1,0:T(8,128)}, u32[]{:S(2)}) copy-start(f32[512,512]{1,0:T(8,128)} %get-tuple-element.117) | copy-start | bytes 3145732
  454.6 262.3 %all-reduce.42.cloned.1.call-start = ((), (), s32[]{:S(2)}) async-start(), calls=%async_computation.8 | async-start | bytes 12582912 | tf_op jit(solution)/shard_map/psum | solution.py:267
  458.8 5.9 copy-start.118
  458.8 5.9 copy-start.119
  458.8 12.3 %copy-start.117 = (f32[512]{0:T(512)S(1)}, f32[512]{0:T(512)}, u32[]{:S(2)}) copy-start(f32[512]{0:T(512)} %get-tuple-element.82) | copy-start | bytes 6148
  458.8 12.3 %copy-start.123 = (f32[128]{0:T(128)S(1)}, f32[128]{0:T(128)}, u32[]{:S(2)}) copy-start(f32[128]{0:T(128)} %get-tuple-element.88) | copy-start | bytes 1540
  458.8 12.3 %copy-start.124 = (f32[128]{0:T(128)S(1)}, f32[128]{0:T(128)}, u32[]{:S(2)}) copy-start(f32[128]{0:T(128)} %get-tuple-element.89) | copy-start | bytes 1540
  (114 other events, 217.0 us)
Sparse Core Ops, SparseCore 0:
  17.1 38.8 all-reduce.25
  93.7 37.4 all-reduce.27
  159.9 32.8 all-reduce.29
  199.7 36.4 all-reduce.31
  244.7 36.4 all-reduce.33
  320.6 32.8 all-reduce.35
  412.5 36.5 all-reduce.37
  454.7 36.6 all-reduce.39
  498.2 218.6 all-reduce.41
where the time goes:
time: 744 us; the launch traced here: 733 us
  waiting for transfers between devices  395 us (53%)
  local copies, waits for them, and re-layouts  102 us (14%)
  blocking collectives  88.3 us (12%)
  other arithmetic  75.2 us (10%)
  matrix products  56 us (8%)
  between operations  16 us (2%)
    psum x1, waiting for transfers between devices, per_device(): lax.psum((gain_grads, early_in_grad, early_back_grad, qkv_grad, pos_grad,...  205 us
    psum x4, waiting for transfers between devices, add_branch(): return base_rows + factor * lax.psum(partial_value, 'tensor')  108 us
    psum x4, waiting for transfers between devices, add_gradient(): cotangent_sum, gain_total = lax.psum((cotangent_in, gain_piece), 'tensor')  81.7 us
    psum x1, blocking collectives, per_device(): lax.psum((gain_grads, early_in_grad, early_back_grad, qkv_grad, pos_grad,...  38.5 us
    dot_general x27, matrix products, matmul(): jnp.dot(first_factor, second_factor, preferred_element_type=jnp.float32)  33.1 us
    another operation x2, other arithmetic  32.2 us
    unnamed x287, local copies, waits for them, and re-layouts  23.3 us
    psum x1, blocking collectives, per_device(): mean_grad, var_grad = lax.psum((mean_grad, var_grad), 'dp')  22 us
  transfers between devices with their start and end apart: 9, of which 8 were waited for; matrix products, arithmetic and copies ran while one was open for 10% of the time, Pallas kernels for 0%

commit v1 on v0

--- a/solution.py
+++ b/solution.py
@@ -3,6 +3,7 @@
 import jax.numpy as jnp
 from jax import lax
 from jax.sharding import PartitionSpec as P
+from jax.lax import all_gather
 
 LENGTH = 512
 EPS = 1e-05
@@ -147,7 +148,11 @@
 
 
 def add_branch(base_rows, partial_value, factor):
-    return base_rows + factor * lax.psum(partial_value, "tensor")
+
+    def heaps_prepare(sample):
+        return all_gather(sample, "tensor").sum(axis=0)
+
+    return base_rows + factor * heaps_prepare(partial_value)
 
 
 def add_gradient(base_rows, cotangent_in, gain_piece):

time: 744 us -> 792 us (1.065)
  local copies, waits for them, and re-layouts: 102 us -> 143 us
  waiting for transfers between devices: 395 us -> 374 us
  other arithmetic: 75.2 us -> 92.2 us
  matrix products: 56 us -> 66.2 us
    psum x4 -> x0, waiting for transfers between devices: 108 us -> none  [add_branch(): return base_rows + factor * lax.psum(partial_value, 'tensor')]
    all_gather x0 -> x4, waiting for transfers between devices: none -> 98.8 us  [heaps_prepare(): return all_gather(sample, 'tensor').sum(axis=0)]
    reduce_sum x0 -> x4, other arithmetic: none -> 14 us  [heaps_prepare(): return all_gather(sample, 'tensor').sum(axis=0)]
    unnamed x287 -> x271, local copies, waits for them, and re-layouts: 23.3 us -> 35.3 us
    psum x4, waiting for transfers between devices: 81.7 us -> 72.3 us  [add_gradient(): cotangent_sum, gain_total = lax.psum((cotangent_in, gain_piece), 'tensor')]
    reduce_sum x0 -> x4, local copies, waits for them, and re-layouts: none -> 7.92 us  [heaps_prepare(): return all_gather(sample, 'tensor').sum(axis=0)]
  transfers between devices with their start and end apart: 9 -> 9, of which waited for: 8 -> 7; matrix products, arithmetic and copies ran while one was open for 10% -> 11% of each run, Pallas kernels for 0% -> 0%
where the time goes in v1:
time: 792 us; the launch traced here: 781 us
  waiting for transfers between devices  374 us (47%)
  local copies, waits for them, and re-layouts  143 us (18%)
  other arithmetic  92.2 us (12%)
  blocking collectives  88.5 us (11%)
  matrix products  66.2 us (8%)
  between operations  15.7 us (2%)
    psum x1, waiting for transfers between devices, per_device(): lax.psum((gain_grads, early_in_grad, early_back_grad, qkv_grad, pos_grad,...  202 us
    all_gather x4, waiting for transfers between devices, heaps_prepare(): return all_gather(sample, 'tensor').sum(axis=0)  98.8 us
    psum x4, waiting for transfers between devices, add_gradient(): cotangent_sum, gain_total = lax.psum((cotangent_in, gain_piece), 'tensor')  72.3 us
    psum x1, blocking collectives, per_device(): lax.psum((gain_grads, early_in_grad, early_back_grad, qkv_grad, pos_grad,...  38 us
    dot_general x27, matrix products, matmul(): jnp.dot(first_factor, second_factor, preferred_element_type=jnp.float32)  36.9 us
    unnamed x271, local copies, waits for them, and re-layouts  35.3 us
    another operation x2, other arithmetic  32.2 us
    psum x1, blocking collectives, per_device(): lax.psum((jnp.sum(mixed_rows, axis=(0, 1)), jnp.sum(mixed_rows * mixed_ro...  22 us
  transfers between devices with their start and end apart: 9, of which 7 were waited for; matrix products, arithmetic and copies ran while one was open for 11% of the time, Pallas kernels for 0%

profile of v1, /device:TPU:0, one launch (start us, length us, event | category | flops | bytes accessed | tf_op | source)
XLA Modules:
  0.0 780.6 jit_solution(9628108663287623607)
XLA Ops:
  14.4 31.0 %fusion.20 = (bf16[1023,256,1]{0,2,1:T(2,128)(2,1)S(1)}, bf16[1023,256,1]{0,2,1:T(2,128)(2,1)S(1)}) fusion(f32[1023]{0:T(1024)S(1)} %subtract_convert_fusion, f32[256]{0:T(256)S(1)} %multiply_exponential_fusion), kind=kLoop, calls=%fused_computation.49 | loop fusion | flops 785664 | bytes 1052668 | tf_op jit(solution)/shard_map/convert.3
  51.7 3.7 reduce_sum.379
  60.1 3.2 pad.50
  63.3 4.9 reshape.456
  68.3 4.9 slice.118
  73.2 6.5 reshape.457
  85.9 3.8 fusion.102
  95.9 35.4 %all-gather.11.cloned.1.call-done = f32[2048,512]{1,0:T(8,128)} async-done(((f32[512,512]{1,0:T(8,128)}), f32[2048,512]{1,0:T(8,128)}) %all-gather.11.cloned.1.call-update) | async-done | bytes 4194320 | tf_op jit(solution)/shard_map/all_gather | solution.py:153
  140.4 22.0 %all-reduce.13 = (f32[128]{0:T(128)}, f32[128]{0:T(128)}) all-reduce(f32[128]{0:T(128)} %get-tuple-element.135, f32[128]{0:T(128)S(1)} %get-tuple-element.134), channel_id=1, replica_groups=mesh['tensor'=4,'dp'=8] {'dp'}, use_global_device_ids=true, to_apply=%region_11.12 | all-reduce | flops 256 | bytes 2048 | tf_op jit(solution)/shard_map/psum | solution.py:206
  173.3 30.9 %all-gather.13.cloned.1.call-done = f32[2048,512]{1,0:T(8,128)} async-done(((f32[512,512]{1,0:T(8,128)}), f32[2048,512]{1,0:T(8,128)}) %all-gather.13.cloned.1.call-update) | async-done | bytes 4194320 | tf_op jit(solution)/shard_map/all_gather | solution.py:153
  204.3 3.7 reduce_sum.394
  218.9 32.5 %all-gather.15.cloned.1.call-done = f32[2048,512]{1,0:T(8,128)} async-done(((f32[512,512]{1,0:T(8,128)}), f32[2048,512]{1,0:T(8,128)}) %all-gather.15.cloned.1.call-update) | async-done | bytes 4194320 | tf_op jit(solution)/shard_map/all_gather | solution.py:153
  251.5 3.7 reduce_sum.400
  285.1 17.7 %all-reduce.22.cloned.1.call-done = f32[512,512]{0,1:T(8,128)} async-done(((f32[512,512]{0,1:T(8,128)}), f32[512,512]{0,1:T(8,128)}) %all-reduce.22.cloned.1.call-update) | async-done | bytes 1048592 | tf_op jit(solution)/shard_map/psum | solution.py:159
  308.4 22.0 %all-reduce.12 = (f32[128]{0:T(128)}, f32[128]{0:T(128)}) all-reduce(f32[128]{0:T(128)} %neg.55, f32[128]{0:T(128)} %multiply_multiply_fusion.5), channel_id=1, replica_groups=mesh['tensor'=4,'dp'=8] {'dp'}, use_global_device_ids=true, to_apply=%region_26.27 | all-reduce | flops 256 | bytes 2048 | tf_op jit(solution)/shard_map/psum | solution.py:230
  358.2 23.8 %all-reduce.24.cloned.1.call-done = f32[512,512]{0,1:T(8,128)} async-done(((f32[512,512]{0,1:T(8,128)}), f32[512,512]{0,1:T(8,128)}) %all-reduce.24.cloned.1.call-update) | async-done | bytes 1048592 | tf_op jit(solution)/shard_map/psum | solution.py:159
  382.0 3.2 fusion.92
  394.7 3.2 pad.53
  397.9 5.1 reshape.463
  403.0 4.9 slice.135
  407.9 6.5 reshape.464
  414.4 3.1 slice.136
  420.4 4.0 fusion.103
  437.3 7.1 reshape.465
  444.4 3.4 pad.57
  447.8 4.2 reshape.466
  452.1 3.3 fusion.12
  466.0 30.8 %all-reduce.26.cloned.1.call-done = f32[512,512]{0,1:T(8,128)} async-done(((f32[512,512]{0,1:T(8,128)}), f32[512,512]{0,1:T(8,128)}) %all-reduce.26.cloned.1.call-update) | async-done | bytes 1048592 | tf_op jit(solution)/shard_map/psum | solution.py:159
  507.7 5.9 fusion.106
  514.6 6.5 all-reduce.15
  521.2 38.0 %all-reduce.11 = (f32[5,512]{1,0:T(8,128)}, f32[2,2,64]{2,1,0:T(2,128)}, f32[31,128]{1,0:T(8,128)}, f32[128]{0:T(128)}, f32[128]{0:T(128)}) all-reduce(f32[5,512]{1,0:T(8,128)S(1)} %stack.27, f32[2,2,64]{2,1,0:T(2,128)S(1)} %pad_add_fusion, f32[31,128]{1,0:T(8,128)S(1)} %bitcast.243, ...), channel_id=1, replica_groups=mesh['tensor'=4,'dp'=8] {'dp'}, use_global_device_ids=true, to_apply=%region_50.51 | all-reduce | flops 7040 | bytes 56320 | tf_op jit(solution)/shard_map/psum | solution.py:272
  562.0 202.5 %all-reduce.30.cloned.1.call-done = (f32[512,512]{1,0:T(8,128)}, f32[512,512]{1,0:T(8,128)}, f32[512,3,128]{2,0,1:T(8,128)}, f32[512,128]{1,0:T(8,128)}, f32[128...) async-done(((f32[512,512]{1,0:T(8,128)}, f32[512,512]{1,0:T(8,128)}, f32[512,3,128]{2,0,1:T(8,128)}, ...) | async-done | bytes 6291472 | tf_op jit(solution)/shard_map/psum | solution.py:272
  (446 shorter events, 183.3 us)
Async XLA Ops:
  7.2 205.9 %copy-start = (bf16[512,512]{1,0:T(8,128)(2,1)S(1)}, bf16[512,512]{1,0:T(8,128)(2,1)}, u32[]{:S(2)}) copy-start(bf16[512,512]{1,0:T(8,128)(2,1)} %param.29) | copy-start | bytes 1572868
  7.2 3.9 copy-start.64
  7.2 44.5 %all-gather.9.cloned.1.call-start = ((), (), s32[]{:S(2)}) async-start(), calls=%async_computation.4 | async-start | bytes 5242880 | tf_op jit(solution)/shard_map/all_gather | solution.py:153
  8.7 3.9 copy-start.78
  14.1 117.2 %all-gather.11.cloned.1.call-start = ((), (), s32[]{:S(2)}) async-start(), calls=%async_computation.5 | async-start | bytes 5242880 | tf_op jit(solution)/shard_map/all_gather | solution.py:153
  14.2 37.0 %copy-start.102 = (f32[2,2,64]{2,1,0:T(2,128)}, f32[2,2,64]{2,1,0:T(2,128)S(1)}, u32[]{:S(2)}) copy-start(f32[2,2,64]{2,1,0:T(2,128)S(1)} %convert_element_type.243) | copy-start | bytes 3076
  48.7 6.7 copy-start.9
  93.9 110.3 %all-gather.13.cloned.1.call-start = ((), (), s32[]{:S(2)}) async-start(), calls=%async_computation.6 | async-start | bytes 5242880 | tf_op jit(solution)/shard_map/all_gather | solution.py:153
  163.7 9.6 %copy-start.103 = (f32[128]{0:T(128)}, f32[128]{0:T(128)S(1)}, u32[]{:S(2)}) copy-start(f32[128]{0:T(128)S(1)} %get-tuple-element.174) | copy-start | bytes 1540
  173.3 78.2 %all-gather.15.cloned.1.call-start = ((), (), s32[]{:S(2)}) async-start(), calls=%async_computation.7 | async-start | bytes 5242880 | tf_op jit(solution)/shard_map/all_gather | solution.py:153
  216.8 86.0 %all-reduce.22.cloned.1.call-start = ((), (), s32[]{:S(2)}) async-start(), calls=%async_computation | async-start | bytes 2097152 | tf_op jit(solution)/shard_map/psum | solution.py:159
  266.6 115.4 %all-reduce.24.cloned.1.call-start = ((), (), s32[]{:S(2)}) async-start(), calls=%async_computation.1 | async-start | bytes 2097152 | tf_op jit(solution)/shard_map/psum | solution.py:159
  267.8 6.9 copy-start.38
  275.5 27.3 %copy-start.8 = (bf16[512,512]{0,1:T(8,128)(2,1)S(1)}, bf16[512,512]{0,1:T(8,128)(2,1)}, u32[]{:S(2)}) copy-start(bf16[512,512]{0,1:T(8,128)(2,1)} %copy.111) | copy-start | bytes 1572868
  302.9 5.0 copy-start.117
  349.0 147.7 %all-reduce.26.cloned.1.call-start = ((), (), s32[]{:S(2)}) async-start(), calls=%async_computation.2 | async-start | bytes 2097152 | tf_op jit(solution)/shard_map/psum | solution.py:159
  351.7 30.3 %copy-start.5 = (f32[512,512]{0,1:T(8,128)S(1)}, f32[512,512]{0,1:T(8,128)}, u32[]{:S(2)}) copy-start(f32[512,512]{0,1:T(8,128)} %copy-done.4) | copy-start | bytes 3145732
  382.0 4.0 copy-start.57
  385.2 5.5 copy-start.10
  460.1 4.7 copy-start.70
  460.2 99.1 %all-reduce.28.cloned.1.call-start = ((), (), s32[]{:S(2)}) async-start(), calls=%async_computation.3 | async-start | bytes 2097152 | tf_op jit(solution)/shard_map/psum | solution.py:159
  466.0 32.7 %copy-start.63 = (bf16[512,512]{1,0:T(8,128)(2,1)S(1)}, bf16[512,512]{1,0:T(8,128)(2,1)}, u32[]{:S(2)}) copy-start(bf16[512,512]{1,0:T(8,128)(2,1)} %param.19) | copy-start | bytes 1572868
  502.2 262.2 %all-reduce.30.cloned.1.call-start = ((), (), s32[]{:S(2)}) async-start(), calls=%async_computation.8 | async-start | bytes 12582912 | tf_op jit(solution)/shard_map/psum | solution.py:272
  507.6 6.0 copy-start.34
  507.6 7.0 copy-start.115
  507.6 7.0 copy-start.116
  507.6 7.0 copy-start.106
  507.6 7.0 copy-start.107
  507.6 7.0 copy-start.108
  507.6 13.5 %copy-start.105 = (f32[512]{0:T(512)S(1)}, f32[512]{0:T(512)}, u32[]{:S(2)}) copy-start(f32[512]{0:T(512)} %get-tuple-element.128) | copy-start | bytes 6148
  507.6 13.6 %copy-start.112 = (f32[128]{0:T(128)S(1)}, f32[128]{0:T(128)}, u32[]{:S(2)}) copy-start(f32[128]{0:T(128)} %get-tuple-element.138) | copy-start | bytes 1540
  507.7 13.6 %copy-start.113 = (f32[128]{0:T(128)S(1)}, f32[128]{0:T(128)}, u32[]{:S(2)}) copy-start(f32[128]{0:T(128)} %get-tuple-element.139) | copy-start | bytes 1540
  (103 other events, 192.1 us)
Sparse Core Ops, SparseCore 0:
  14.2 37.1 all-gather.8
  94.0 37.1 all-gather.10
  173.4 30.7 all-gather.12
  216.9 34.4 all-gather.14
  266.7 36.0 all-reduce.21
  349.1 32.8 all-reduce.23
  460.3 36.4 all-reduce.25
  502.3 36.4 all-reduce.27
  545.7 218.6 all-reduce.29
